TPU v7x, 32 devices: a whole 2x2x4 slice. The times are simulated.
32 devices in a mesh: seq: 8 (over z, x), chan: 4 (over y, core).
Axes of the slice: x: 2, y: 2, z: 4, core: 2. Of those that a mesh axis runs over, the one named last changes fastest.
Arguments:
- projected: bfloat16 [3, 2048, 2048], P(None, 'seq', 'chan'), may hold values from -6 to 6
- short_taps: float32 [3, 3, 2048], P(None, None, 'chan'), may hold values from -3 to 3
- skip_gain: float32 [2048], P('chan'), may hold values from 0.5 to 1.5
- filter_response: float32 [2, 4096, 2048], P(None, 'seq', 'chan'), may hold values from -6 to 6
- out_weight: bfloat16 [2048, 8192], P('chan'), may hold values from -0.1875 to 0.1875
Outputs:
- mixed: bfloat16 [2048, 8192], P('seq', 'chan')
All inputs are finite; a program needn't handle non-finite values.
Results may differ from a plain program's by a relative error of at most 0.015.
Values may be sent and summed in bfloat16 or wider, within the bound.
A program may use at most 64 MiB of HBM per device.

v0:
```python
import math

import jax
import jax.numpy as jnp
from jax import lax
from jax.sharding import PartitionSpec as P


def shifted(value, axis, steps):
    count = lax.axis_size(axis)
    first, last = (max(0, -steps), min(count, count - steps))
    return lax.ppermute(value, axis, [(source, source + steps) for source in range(first, last)])


def product_einsum(form, left, right):
    return jnp.einsum(form, left, right, precision=lax.Precision.HIGHEST)


def per_device(projected, short_taps, skip_gain, filter_response, out_weight):
    seq_rows = projected.shape[1]
    seq_parts = lax.axis_size("seq")
    coarse_len = 2 * seq_parts
    total_len = coarse_len * seq_rows
    rim_rows = shifted(projected[:, seq_rows - 2 :, :], "seq", 1)
    padded = jnp.concatenate([rim_rows, projected], axis=1).astype(jnp.float32)
    shaped = (
        short_taps[:, 0, None, :] * padded[:, 2:]
        + short_taps[:, 1, None, :] * padded[:, 1:-1]
        + short_taps[:, 2, None, :] * padded[:, :-2]
    )
    query = shaped[0]
    signal = shaped[1] * shaped[2]
    coarse_freq = jnp.arange(coarse_len, dtype=jnp.int32)
    coarse_pos = jnp.arange(seq_parts, dtype=jnp.int32)
    coarse_angle = (
        2.0
        * math.pi
        / coarse_len
        * (coarse_freq[:, None] * coarse_pos[None, :] % coarse_len).astype(jnp.float32)
    )
    coarse_cos = jnp.cos(coarse_angle)
    coarse_sin = jnp.sin(coarse_angle)
    fine_index = jnp.arange(seq_rows, dtype=jnp.int32)
    fine_angle = (
        2.0
        * math.pi
        / seq_rows
        * (fine_index[:, None] * fine_index[None, :] % seq_rows).astype(jnp.float32)
    )
    fine_cos = jnp.cos(fine_angle)
    fine_sin = jnp.sin(fine_angle)
    narrow = lax.all_to_all(
        signal.astype(jnp.bfloat16), "seq", split_axis=1, concat_axis=0, tiled=True
    ).astype(signal.dtype)
    resp_narrow = lax.all_to_all(
        filter_response.astype(jnp.bfloat16), "seq", split_axis=2, concat_axis=1, tiled=True
    ).astype(filter_response.dtype)
    narrow_width = narrow.shape[1]
    blocks = narrow.reshape(seq_parts, seq_rows, narrow_width)
    whole_angle = (
        2.0
        * math.pi
        / total_len
        * (coarse_freq[:, None] * fine_index[None, :] % total_len).astype(jnp.float32)
    )
    whole_cos = jnp.cos(whole_angle)[:, :, None]
    whole_sin = jnp.sin(whole_angle)[:, :, None]
    first_real = product_einsum("kn,nrc->krc", coarse_cos, blocks)
    first_imag = -product_einsum("kn,nrc->krc", coarse_sin, blocks)
    turned_real = first_real * whole_cos + first_imag * whole_sin
    turned_imag = first_imag * whole_cos - first_real * whole_sin
    spec_real = product_einsum("kn,jnc->kjc", fine_cos, turned_real) + product_einsum(
        "kn,jnc->kjc", fine_sin, turned_imag
    )
    spec_imag = product_einsum("kn,jnc->kjc", fine_cos, turned_imag) - product_einsum(
        "kn,jnc->kjc", fine_sin, turned_real
    )
    resp_grid = resp_narrow.reshape(2, seq_rows, coarse_len, narrow_width)
    kept_real = spec_real * resp_grid[0] - spec_imag * resp_grid[1]
    kept_imag = spec_real * resp_grid[1] + spec_imag * resp_grid[0]
    back_real = product_einsum("kn,kjc->jnc", fine_cos, kept_real) - product_einsum(
        "kn,kjc->jnc", fine_sin, kept_imag
    )
    back_imag = product_einsum("kn,kjc->jnc", fine_cos, kept_imag) + product_einsum(
        "kn,kjc->jnc", fine_sin, kept_real
    )
    untwist_real = back_real * whole_cos - back_imag * whole_sin
    untwist_imag = back_real * whole_sin + back_imag * whole_cos
    inverse_part = (
        product_einsum("kn,krc->nrc", coarse_cos, untwist_real)
        - product_einsum("kn,krc->nrc", coarse_sin, untwist_imag)
    ) * (1.0 / total_len)
    filtered = lax.all_to_all(
        inverse_part.reshape(seq_parts * seq_rows, narrow_width).astype(jnp.bfloat16),
        "seq",
        split_axis=0,
        concat_axis=1,
        tiled=True,
    ).astype(jnp.float32)
    gated = (query * (filtered + skip_gain[None, :] * signal)).astype(jnp.bfloat16)
    partial_terms = jnp.dot(gated, out_weight, preferred_element_type=jnp.float32)
    return lax.psum_scatter(
        partial_terms.astype(jnp.bfloat16), "chan", scatter_dimension=1, tiled=True
    )


def solution(mesh):
    placed = (
        P(None, "seq", "chan"),
        P(None, None, "chan"),
        P("chan"),
        P(None, "seq", "chan"),
        P("chan", None),
    )
    return jax.shard_map(
        per_device, mesh=mesh, in_specs=placed, out_specs=P("seq", "chan"), check_vma=False
    )
```

profile of v0, /device:TPU:0, one launch (start us, length us, event | category | flops | bytes accessed | tf_op | source)
XLA Modules:
  0.0 162.8 jit_solution(2009303027244785898)
XLA Ops:
  6.5 0.7 slice.43
  7.6 4.9 %collective-permute-start = (bf16[3,2,512]{1,2,0:T(8,128)(2,1)S(1)}, bf16[3,2,512]{1,2,0:T(8,128)(2,1)S(1)}, u32[]{:S(2)}, u32[]{:S(2)}) collective-permute-start(bf16[3,2,512]{1,2,0:T(8,128)(2,1)S(1)} %copy.29), channel_id=1, source_target_pairs={{0,4},{4,8},{8,12},{12,16},{16,20},{20,24},{24,28},{1,5},{5,9},{9,... | collective-permute-start | bytes 18440 | tf_op jit(solution)/shard_map/ppermute | solution.py:12
  12.4 0.9 fusion.114
  13.3 1.4 copy.30
  14.7 6.0 %collective-permute-done = bf16[3,2,512]{1,2,0:T(8,128)(2,1)S(1)} collective-permute-done((bf16[3,2,512]{1,2,0:T(8,128)(2,1)S(1)}, bf16[3,2,512]{1,2,0:T(8,128)(2,1)S(1)}, u32[]{:S(2)}, u32[]{:S(2)}) %collective-permute-start) | collective-permute-done | bytes 6176 | tf_op jit(solution)/shard_map/ppermute | solution.py:12
  21.3 1.6 fusion
  22.9 0.8 fusion.26
  23.7 6.8 %all-to-all-start = ((bf16[256,8,64]{0,2,1:T(8,128)(2,1)}), bf16[256,8,64]{0,2,1:T(8,128)(2,1)S(1)}, u32[]{:S(2)}, u32[]{:S(2)}) async-start(bf16[256,8,64]{0,2,1:T(8,128)(2,1)} %bitcast.2), calls=%async_computation | async-start | bytes 524288 | tf_op jit(solution)/shard_map/all_to_all | solution.py:52
  30.5 4.0 %copy.34 = bf16[2,512,512]{1,0,2:T(2,128)(2,1)} copy(f32[2,512,512]{2,1,0:T(8,128)} %param.8) | data formatting | bytes 3145728 | tf_op args[3]
  34.4 4.2 %all-to-all-done = bf16[256,8,64]{0,2,1:T(8,128)(2,1)S(1)} async-done(((bf16[256,8,64]{0,2,1:T(8,128)(2,1)}), bf16[256,8,64]{0,2,1:T(8,128)(2,1)S(1)}, u32[]{:S(2)}, u32[]{:S(2)}) %all-to-all-start) | async-done | bytes 262176 | tf_op jit(solution)/shard_map/all_to_all | solution.py:52
  38.7 3.6 %all-to-all-start.1 = ((bf16[2,512,512]{1,0,2:T(2,128)(2,1)}), bf16[2,512,512]{1,0,2:T(2,128)(2,1)S(1)}, u32[]{:S(2)}, u32[]{:S(2)}) async-start(bf16[2,512,512]{1,0,2:T(2,128)(2,1)} %copy.34), calls=%async_computation.1 | async-start | bytes 2097152 | tf_op jit(solution)/shard_map/all_to_all | solution.py:55
  43.3 0.9 multiply_add_fusion.1
  45.4 3.0 %fusion.37 = f32[256,1024]{0,1} fusion(f32[256,1024]{0,1:T(8,128)S(1)} %bitcast.91), kind=kOutput, calls=%fused_computation.54 | convolution fusion | flops 806223872 | bytes 2097152
  48.4 3.0 %fusion.33 = f32[256,1024]{0,1} fusion(f32[256,1024]{0,1:T(8,128)S(1)} %bitcast.92), kind=kOutput, calls=%fused_computation.53 | convolution fusion | flops 806223872 | bytes 2097152
  51.3 3.0 %fusion.31 = f32[256,1024]{0,1} fusion(f32[256,1024]{0,1:T(8,128)S(1)} %bitcast.89), kind=kOutput, calls=%fused_computation.52 | convolution fusion | flops 806223872 | bytes 2097152
  54.3 3.0 %fusion.39 = f32[256,1024]{0,1} fusion(f32[256,1024]{0,1:T(8,128)S(1)} %bitcast.90), kind=kOutput, calls=%fused_computation.55 | convolution fusion | flops 806223872 | bytes 2097152
  57.3 10.1 %all-to-all-done.1 = bf16[2,512,512]{1,0,2:T(2,128)(2,1)S(1)} async-done(((bf16[2,512,512]{1,0,2:T(2,128)(2,1)}), bf16[2,512,512]{1,0,2:T(2,128)(2,1)S(1)}, u32[]{:S(2)}, u32[]{:S(2)}) %all-to-all-start.1) | async-done | bytes 1048608 | tf_op jit(solution)/shard_map/all_to_all | solution.py:55
  67.9 1.2 fusion.113
  69.1 3.2 %copy.40 = f32[1,8,512,64]{3,2,1,0:T(8,128)} copy(f32[1,8,512,64]{2,3,1,0:T(8,128)} %get-tuple-element.11) | data formatting | bytes 2097152 | tf_op jit(solution)/shard_map/slice | solution.py:79
  72.2 3.7 %copy.41 = f32[256,16,64]{0,2,1:T(8,128)} copy(f32[256,16,64]{2,1,0:T(8,128)} %bitcast.93) | data formatting | bytes 2097152 | tf_op jit(solution)/shard_map/squeeze | solution.py:79
  75.9 1.9 %copy.36 = f32[1,8,512,64]{3,2,1,0:T(8,128)} copy(f32[1,8,512,64]{2,3,1,0:T(8,128)S(1)} %get-tuple-element.12) | data formatting | bytes 2097152 | tf_op jit(solution)/shard_map/slice | solution.py:79
  77.9 3.6 %copy.37 = f32[256,16,64]{0,2,1:T(8,128)} copy(f32[256,16,64]{2,1,0:T(8,128)} %bitcast.94) | data formatting | bytes 2097152 | tf_op jit(solution)/shard_map/squeeze | solution.py:79
  81.4 3.1 %multiply_subtract_fusion = (f32[256,16,64]{0,2,1:T(8,128)S(1)}, f32[256,16,64]{0,2,1:T(8,128)S(1)}) fusion(f32[256,16,64]{0,2,1:T(8,128)S(1)} %copy-done, f32[256,16,64]{0,2,1:T(8,128)} %copy.37, f32[256,16,64]{0,2,1:T(8,128)} %bitcast.100, f32[256,16,64]{0,2,1:T(8,128)} %bitcast.98, f32[256,16,64]{0,2,1:T(8,128)} %bitcast.99, f32[256,16,64]{0,2,1:T(8,128)} %bitcast.101), kind=kLoop, calls=%fused_computation.20 | loop fusion | flops 2097152 | bytes 8388608 | tf_op jit(solution)/shard_map/sub | solution.py:79
  84.5 2.0 %fusion.14 = f32[16,64,256]{2,1,0:T(8,128)S(1)} fusion(f32[256,16,64]{0,2,1:T(8,128)S(1)} %get-tuple-element.6), kind=kOutput, calls=%fused_computation.37 | convolution fusion | flops 806223872 | bytes 2097152 | tf_op jit(solution)/shard_map/kn,kjc->jnc/dot_general | solution.py:16
  86.5 2.0 %fusion.16 = f32[16,64,256]{2,1,0:T(8,128)S(1)} fusion(f32[256,16,64]{0,2,1:T(8,128)S(1)} %get-tuple-element.5), kind=kOutput, calls=%fused_computation.39 | convolution fusion | flops 806223872 | bytes 2097152 | tf_op jit(solution)/shard_map/kn,kjc->jnc/dot_general | solution.py:16
  88.5 2.0 %convolution_add_fusion = f32[16,64,256]{2,1,0:T(8,128)S(1)} fusion(f32[16,64,256]{2,1,0:T(8,128)S(1)} %fusion.14, f32[256,16,64]{0,2,1:T(8,128)S(1)} %get-tuple-element.5), kind=kOutput, calls=%fused_computation.8 | convolution fusion | flops 806486016 | bytes 3145728 | tf_op jit(solution)/shard_map/kn,kjc->jnc/dot_general | solution.py:16
  90.4 2.1 %add_bitcast_fusion = (f32[16,256,64]{1,2,0:T(8,128)S(1)}, f32[16,256,64]{1,2,0:T(8,128)S(1)}) fusion(f32[16,64,256]{2,1,0:T(8,128)S(1)} %convolution_add_fusion, f32[16,256]{1,0:T(8,128)S(1)} %get-tuple-element.18, f32[16,256]{1,0:T(8,128)S(1)} %get-tuple-element.19, f32[16,64,256]{2,1,0:T(8,128)S(1)} %fusion.16, f32[256,16,64]{0,2,1:T(8,128)S(1)} %get-tuple-element.6), kind=kOutput, calls=%fused_computation.17 | convolution fusion | flops 808058880 | bytes 5275648 | tf_op jit(solution)/shard_map/kn,kjc->jnc/dot_general | solution.py:16
  92.5 1.5 fusion.5
  94.0 1.2 fusion.3
  95.3 12.3 %all_to_all.32 = bf16[8,256,64]{1,2,0:T(8,128)(2,1)S(1)} all-to-all(bf16[8,256,64]{1,2,0:T(8,128)(2,1)S(1)} %copy.46), channel_id=1, replica_groups=mesh['seq'=8,'chan'=4] {'seq'}, dimensions={0} | all-to-all | bytes 524288 | tf_op jit(solution)/shard_map/all_to_all | solution.py:93
  107.8 4.5 %convolution_convert_fusion = bf16[256,8192]{1,0:T(8,128)(2,1)} fusion(bf16[256,512]{0,1:T(8,128)(2,1)S(1)} %fusion.8, bf16[512,8192]{1,0:T(8,128)(2,1)S(1)} %bitcast.96), kind=kOutput, calls=%fused_computation | convolution fusion | flops 2149580800 | bytes 12845056 | tf_op jit(solution)/shard_map/dot_general | solution.py:101
  112.3 43.7 %reduce-scatter.2.cloned.1.call-done = bf16[256,2048]{1,0:T(8,128)(2,1)} async-done(((bf16[256,8192]{1,0:T(8,128)(2,1)}), bf16[256,2048]{1,0:T(8,128)(2,1)}) %reduce-scatter.2.cloned.1.call-update) | async-done | bytes 1048592 | tf_op jit(solution)/shard_map/reduce_scatter | solution.py:102
  (23 shorter events, 3.7 us)
Async XLA Ops:
  7.6 13.2 %collective-permute-start = (bf16[3,2,512]{1,2,0:T(8,128)(2,1)S(1)}, bf16[3,2,512]{1,2,0:T(8,128)(2,1)S(1)}, u32[]{:S(2)}, u32[]{:S(2)}) collective-permute-start(bf16[3,2,512]{1,2,0:T(8,128)(2,1)S(1)} %copy.29), channel_id=1, source_target_pairs={{0,4},{4,8},{8,12},{12,16},{16,20},{20,24},{24,28},{1,5},{5,9},{9,... | collective-permute-start | bytes 18440 | tf_op jit(solution)/shard_map/ppermute | solution.py:12
  23.7 15.0 %all-to-all-start = ((bf16[256,8,64]{0,2,1:T(8,128)(2,1)}), bf16[256,8,64]{0,2,1:T(8,128)(2,1)S(1)}, u32[]{:S(2)}, u32[]{:S(2)}) async-start(bf16[256,8,64]{0,2,1:T(8,128)(2,1)} %bitcast.2), calls=%async_computation | async-start | bytes 524288 | tf_op jit(solution)/shard_map/all_to_all | solution.py:52
  38.7 28.7 %all-to-all-start.1 = ((bf16[2,512,512]{1,0,2:T(2,128)(2,1)}), bf16[2,512,512]{1,0,2:T(2,128)(2,1)S(1)}, u32[]{:S(2)}, u32[]{:S(2)}) async-start(bf16[2,512,512]{1,0,2:T(2,128)(2,1)} %copy.34), calls=%async_computation.1 | async-start | bytes 2097152 | tf_op jit(solution)/shard_map/all_to_all | solution.py:55
  42.3 113.7 %reduce-scatter.2.cloned.1.call-start = ((), (), s32[]{:S(2)}) async-start(), calls=%async_computation.4 | async-start | bytes 5242880 | tf_op jit(solution)/shard_map/reduce_scatter | solution.py:102
  77.9 3.6 %copy-start = (f32[256,16,64]{0,2,1:T(8,128)S(1)}, f32[256,16,64]{0,2,1:T(8,128)}, u32[]{:S(2)}) copy-start(f32[256,16,64]{0,2,1:T(8,128)} %copy.41) | copy-start | bytes 3145732
  86.5 21.3 %slice-start = ((s8[8388608]{0:T(1024)(128)(4,1)}), s8[4194304]{0:T(1024)(128)(4,1)S(1)}, s32[]{:S(2)}) async-start(s8[8388608]{0:T(1024)(128)(4,1)} %bitcast.95), calls=%async_computation.5 | async-start | bytes 8388608
  90.4 17.3 %slice-start.1 = ((s8[8388608]{0:T(1024)(128)(4,1)}), s8[4194304]{0:T(1024)(128)(4,1)S(1)}, s32[]{:S(2)}) async-start(s8[8388608]{0:T(1024)(128)(4,1)} %bitcast.95), calls=%async_computation.6 | async-start | bytes 8388608
  92.5 15.0 %copy-start.1 = (f32[512]{0:T(512)S(1)}, f32[512]{0:T(512)}, u32[]{:S(2)}) copy-start(f32[512]{0:T(512)} %param.7) | copy-start | bytes 6148
Sparse Core Ops, SparseCore 0:
  112.4 43.5 reduce-scatter.1
where the time goes:
time: 163 us
  waiting for transfers between devices  64.1 us (39%)
  matrix products  28.6 us (18%)
  local copies, waits for them, and re-layouts  22.3 us (14%)
  starting transfers between devices  15.4 us (9%)
  between operations  13.6 us (8%)
  blocking collectives  12.3 us (8%)
  other arithmetic  6.52 us (4%)
    reduce_scatter x1, waiting for transfers between devices, per_device(): lax.psum_scatter(partial_terms.astype(jnp.bfloat16), 'chan', scatter_dime...  43.7 us
    all_to_all x1, blocking collectives, per_device(): lax.all_to_all(inverse_part.reshape(seq_parts * seq_rows, narrow_width).a...  12.3 us
    dot_general x8, matrix products, product_einsum(): return jnp.einsum(form, left, right, precision=lax.Precision.HIGHEST)  12.2 us
    unnamed x4, matrix products  11.9 us
    all_to_all x1, waiting for transfers between devices, per_device(): lax.all_to_all(filter_response.astype(jnp.bfloat16), 'seq', split_axis=2,...  10.1 us
    squeeze x2, local copies, waits for them, and re-layouts, per_device(): kept_real = spec_real * resp_grid[0] - spec_imag * resp_grid[1]  7.24 us
    all_to_all x1, starting transfers between devices, per_device(): lax.all_to_all(signal.astype(jnp.bfloat16), 'seq', split_axis=1, concat_a...  6.8 us
    slice x3, local copies, waits for them, and re-layouts, per_device(): kept_real = spec_real * resp_grid[0] - spec_imag * resp_grid[1]  6.31 us
  transfers between devices with their start and end apart: 4, of which 4 were waited for; matrix products, arithmetic and copies ran while one was open for 13% of the time, Pallas kernels for 0%

commit v1 on v0

--- a/solution.py
+++ b/solution.py
@@ -1,9 +1,374 @@
+import functools
 import math
 
 import jax
 import jax.numpy as jnp
+import numpy as np
 from jax import lax
+from jax.experimental import pallas as pl
+from jax.experimental.pallas import tpu as pltpu
 from jax.sharding import PartitionSpec as P
+
+LANES = 128
+MESH = pl.DeviceIdType.MESH
+
+
+def dft_tables(rows, parts):
+    coarse = 2 * parts
+    total = coarse * rows
+    half = rows // 2
+    r = np.arange(rows)[None, :]
+    k = np.arange(half)[:, None]
+
+    def pair(j):
+        angle = 2.0 * np.pi * ((r * (coarse * k + j)) % total) / total
+        return np.cos(angle), np.sin(angle)
+
+    tables = np.zeros((parts, 2 * rows, 2 * rows), np.float32)
+    cos0, sin0 = pair(0)
+    cosn, sinn = pair(parts)
+    tables[0, :half, :rows] = cos0
+    tables[0, half:rows, :rows] = -sin0
+    tables[0, rows : rows + half, rows:] = cosn
+    tables[0, rows + half :, rows:] = -sinn
+    for m in range(1, parts):
+        c, s = pair(m)
+        tables[m, :rows] = np.block([[c, s], [-s, c]])
+        c, s = pair(coarse - m)
+        tables[m, rows:] = np.block([[c, -s], [-s, -c]])
+    return tables.astype(jnp.bfloat16)
+
+
+def regroup_matrix(count, coarse):
+    fine = count // coarse
+    matrix = np.zeros((count, count), np.float32)
+    out = np.arange(count)
+    matrix[out, (out % fine) * coarse + out // fine] = 1.0
+    return matrix.astype(jnp.bfloat16)
+
+
+def weighted(terms):
+    total = None
+    for weight, value in terms:
+        if abs(weight) < 1e-12:
+            continue
+        if abs(weight - 1.0) < 1e-12:
+            part = value
+        elif abs(weight + 1.0) < 1e-12:
+            part = -value
+        else:
+            part = value * weight
+        total = part if total is None else total + part
+    return total
+
+
+def layer_kernel(
+    parts, pieces,
+    proj_hbm, taps_ref, skip_ref, filt_hbm, weight_hbm, tables_hbm, regroup_ref,
+    out_ref,
+    proj, filt, weight, tables, rim,
+    query, signal, signal_bf, heard, filt_bf, resp,
+    coarse_in, spectrum, inverse, narrow_out, returned, gated,
+    side_out, side_in, far_out, far_in, side_own_out, side_own_in,
+    load_sem, rim_sem, sig_send, sig_recv, filt_send, filt_recv,
+    back_send, back_recv, side_send, side_recv, far_send, far_recv, own_send, own_recv,
+):
+    seq = lax.axis_index("seq")
+    chan = lax.axis_index("chan")
+    groups = parts // 2
+    half = seq // groups
+    group = seq % groups
+    sibling = chan + 1 - 2 * (chan % 2)
+    across = (chan + 2) % 4
+    diagonal = (sibling + 2) % 4
+    rows = proj.shape[1]
+    coarse = 2 * parts
+    half_rows = rows // 2
+    fine_held = filt.shape[1] // coarse
+    out_width = out_ref.shape[1]
+    piece = out_width // pieces
+
+    load_proj = pltpu.make_async_copy(proj_hbm, proj, load_sem.at[0])
+    load_proj.start()
+    load_filt = []
+    for p in range(2):
+        load_filt.append(pltpu.make_async_copy(filt_hbm.at[p], filt.at[p], load_sem.at[1 + p]))
+        load_filt[-1].start()
+    load_tables = pltpu.make_async_copy(tables_hbm, tables, load_sem.at[3])
+    load_tables.start()
+    load_weight = pltpu.make_async_copy(weight_hbm, weight, load_sem.at[4])
+    load_weight.start()
+
+    barrier = pltpu.get_barrier_semaphore()
+    for o in range(1, parts):
+        pl.semaphore_signal(barrier, inc=1, device_id={"seq": (seq + o) % parts}, device_id_type=MESH)
+    for partner in (sibling, across):
+        pl.semaphore_signal(barrier, inc=1, device_id={"chan": partner}, device_id_type=MESH)
+    pl.semaphore_wait(barrier, parts + 1)
+
+    load_proj.wait()
+    rim_copy = pltpu.make_async_remote_copy(
+        src_ref=proj.at[:, pl.ds(rows - 16, 16), :],
+        dst_ref=rim,
+        send_sem=rim_sem.at[0],
+        recv_sem=rim_sem.at[1],
+        device_id={"seq": (seq + 1) % parts},
+        device_id_type=MESH,
+    )
+    rim_copy.start()
+
+    filt_copies = []
+
+    def send_filter(p):
+        load_filt[p].wait()
+        filt_bf[p] = jnp.dot(
+            regroup_ref[...], filt[p].astype(jnp.bfloat16), preferred_element_type=jnp.float32
+        ).astype(jnp.bfloat16)
+        for o in range(1, groups):
+            target = (group + o) % groups
+            columns = pl.ds(pl.multiple_of(target * LANES, LANES), LANES)
+            copy = pltpu.make_async_remote_copy(
+                src_ref=filt_bf.at[p, :, columns],
+                dst_ref=resp.at[group, p],
+                send_sem=filt_send.at[p, o],
+                recv_sem=filt_recv.at[p, o],
+                device_id={"seq": half * groups + target},
+                device_id_type=MESH,
+            )
+            copy.start()
+            filt_copies.append(copy)
+
+    send_filter(0)
+    rim_copy.wait()
+
+    row_index = lax.broadcasted_iota(jnp.int32, (rows, LANES), 0)
+
+    def shaped(i, columns):
+        now = proj[i, :, columns].astype(jnp.float32)
+        edge = rim[i, :, columns].astype(jnp.float32)
+        edge = jnp.where(seq == 0, jnp.zeros_like(edge), edge)
+        last, before = edge[15:16], edge[14:15]
+        one = jnp.where(row_index == 0, last, pltpu.roll(now, 1, 0))
+        two = jnp.where(row_index == 0, before, jnp.where(row_index == 1, last, pltpu.roll(now, 2, 0)))
+        return (
+            taps_ref[3 * i : 3 * i + 1, columns] * now
+            + taps_ref[3 * i + 1 : 3 * i + 2, columns] * one
+            + taps_ref[3 * i + 2 : 3 * i + 3, columns] * two
+        )
+
+    for g in range(groups):
+        columns = slice(g * LANES, (g + 1) * LANES)
+        product = shaped(1, columns) * shaped(2, columns)
+        signal[:, columns] = product
+        signal_bf[:, columns] = product.astype(jnp.bfloat16)
+
+    own_columns = pl.ds(pl.multiple_of(group * LANES, LANES), LANES)
+    sig_copies = []
+    for o in range(1, parts):
+        target = (seq + o) % parts
+        columns = pl.ds(pl.multiple_of((target % groups) * LANES, LANES), LANES)
+        copy = pltpu.make_async_remote_copy(
+            src_ref=signal_bf.at[:, columns],
+            dst_ref=heard.at[seq],
+            send_sem=sig_send.at[o],
+            recv_sem=sig_recv.at[o],
+            device_id={"seq": target},
+            device_id_type=MESH,
+        )
+        copy.start()
+        sig_copies.append(copy)
+    heard[seq] = signal_bf[:, own_columns]
+    send_filter(1)
+    for p in range(2):
+        resp[group, p] = filt_bf[p, :, own_columns]
+    for g in range(groups):
+        columns = slice(g * LANES, (g + 1) * LANES)
+        query[:, columns] = shaped(0, columns)
+
+    for copy in sig_copies:
+        copy.wait_recv()
+
+    chunk = 32
+
+    def parity(start):
+        index = lax.broadcasted_iota(jnp.int32, (chunk, LANES), 0)
+        return (1 - 2 * half * (index % 2)).astype(jnp.float32)
+
+    angle = 2.0 * math.pi / coarse
+
+    def forward(step, carry):
+        start = pl.multiple_of(step * chunk, chunk)
+        sign = parity(start)
+        x = [heard[n, pl.ds(start, chunk), :].astype(jnp.float32) * sign for n in range(parts)]
+        for m in range(parts):
+            if m == 0:
+                real = weighted([(1.0, x[n]) for n in range(parts)])
+                imag = weighted([((-1.0) ** n, x[n]) for n in range(parts)])
+            else:
+                real = weighted([(math.cos(angle * m * n), x[n]) for n in range(parts)])
+                imag = weighted([(-math.sin(angle * m * n), x[n]) for n in range(parts)])
+            coarse_in[m, pl.ds(start, chunk), :] = real.astype(jnp.bfloat16)
+            coarse_in[m, pl.ds(rows + start, chunk), :] = imag.astype(jnp.bfloat16)
+        return carry
+
+    lax.fori_loop(0, rows // chunk, forward, 0)
+    load_tables.wait()
+    for m in range(parts):
+        spectrum[m] = jnp.dot(tables[m], coarse_in[m], preferred_element_type=jnp.float32)
+
+    for copy in filt_copies:
+        copy.wait_recv()
+
+    for m in range(parts):
+        kept = []
+        for at, j in ((0, m), (rows, parts if m == 0 else coarse - m)):
+            real = spectrum[m, at : at + half_rows]
+            imag = spectrum[m, at + half_rows : at + rows]
+            held = slice(j * fine_held, (j + 1) * fine_held)
+            resp_real = jnp.concatenate([resp[g, 0, held] for g in range(groups)], 0).astype(jnp.float32)
+            resp_imag = jnp.concatenate([resp[g, 1, held] for g in range(groups)], 0).astype(jnp.float32)
+            kept.append((real * resp_real - imag * resp_imag).astype(jnp.bfloat16))
+            kept.append((real * resp_imag + imag * resp_real).astype(jnp.bfloat16))
+        inverse[m] = lax.dot_general(
+            tables[m], jnp.concatenate(kept, 0), (((0,), (0,)), ((), ())), preferred_element_type=jnp.float32
+        )
+
+    def backward(step, carry):
+        start = pl.multiple_of(step * chunk, chunk)
+        sign = parity(start) * (1.0 / (coarse * rows))
+        real = [inverse[m, pl.ds(start, chunk), :] for m in range(parts)]
+        imag = [inverse[m, pl.ds(rows + start, chunk), :] for m in range(parts)]
+        for n in range(parts):
+            terms = [(1.0, real[0]), ((-1.0) ** n, imag[0])]
+            for m in range(1, parts):
+                terms.append((math.cos(angle * m * n), real[m]))
+                terms.append((-math.sin(angle * m * n), imag[m]))
+            narrow_out[n, pl.ds(start, chunk), :] = (weighted(terms) * sign).astype(jnp.bfloat16)
+        return carry
+
+    lax.fori_loop(0, rows // chunk, backward, 0)
+    back_copies = []
+    for o in range(1, parts):
+        target = (seq + o) % parts
+        copy = pltpu.make_async_remote_copy(
+            src_ref=narrow_out.at[target],
+            dst_ref=returned.at[seq],
+            send_sem=back_send.at[o],
+            recv_sem=back_recv.at[o],
+            device_id={"seq": target},
+            device_id_type=MESH,
+        )
+        copy.start()
+        back_copies.append(copy)
+    returned[seq] = narrow_out[seq]
+    load_weight.wait()
+    for copy in back_copies:
+        copy.wait_recv()
+
+    for g in range(groups):
+        columns = slice(g * LANES, (g + 1) * LANES)
+        filtered = returned[g].astype(jnp.float32) + returned[groups + g].astype(jnp.float32)
+        gated[:, columns] = (
+            query[:, columns] * (filtered + skip_ref[:, columns] * signal[:, columns])
+        ).astype(jnp.bfloat16)
+
+    def product(block, c):
+        columns = pl.ds(pl.multiple_of(block * out_width + c * piece, piece), piece)
+        return jnp.dot(gated[...], weight[:, columns], preferred_element_type=jnp.float32)
+
+    def send(source, target_ref, send_sem, recv_sem, c, partner):
+        copy = pltpu.make_async_remote_copy(
+            src_ref=source.at[c],
+            dst_ref=target_ref.at[c],
+            send_sem=send_sem.at[c],
+            recv_sem=recv_sem.at[c],
+            device_id={"chan": partner},
+            device_id_type=MESH,
+        )
+        copy.start()
+        return copy
+
+    side_copies, far_copies, own_copies = [], [], []
+    for c in range(pieces):
+        side_out[c] = product(diagonal, c).astype(jnp.bfloat16)
+        side_copies.append(send(side_out, side_in, side_send, side_recv, c, sibling))
+    for c in range(pieces):
+        mine = product(across, c)
+        side_copies[c].wait_recv()
+        far_out[c] = (mine + side_in[c].astype(jnp.float32)).astype(jnp.bfloat16)
+        far_copies.append(send(far_out, far_in, far_send, far_recv, c, across))
+    for c in range(pieces):
+        side_own_out[c] = product(sibling, c).astype(jnp.bfloat16)
+        own_copies.append(send(side_own_out, side_own_in, own_send, own_recv, c, sibling))
+    for c in range(pieces):
+        mine = product(chan, c)
+        own_copies[c].wait_recv()
+        far_copies[c].wait_recv()
+        out_ref[:, c * piece : (c + 1) * piece] = (
+            mine + side_own_in[c].astype(jnp.float32) + far_in[c].astype(jnp.float32)
+        ).astype(jnp.bfloat16)
+    for copy in filt_copies + sig_copies + back_copies + side_copies + far_copies + own_copies:
+        copy.wait_send()
+
+
+def per_device_kernel(projected, short_taps, skip_gain, filter_response, out_weight):
+    parts = lax.axis_size("seq")
+    chans = lax.axis_size("chan")
+    rows, width = projected.shape[1:]
+    held = filter_response.shape[1]
+    out_width = out_weight.shape[1] // chans
+    groups = parts // 2
+    pieces = 4
+    piece = out_width // pieces
+    bf, f32 = jnp.bfloat16, jnp.float32
+    any_spec = pl.BlockSpec(memory_space=pl.ANY)
+    vmem_spec = pl.BlockSpec(memory_space=pltpu.VMEM)
+    dma = pltpu.SemaphoreType.DMA
+    exchange = pltpu.VMEM((pieces, rows, piece), bf)
+    return pl.pallas_call(
+        functools.partial(layer_kernel, parts, pieces),
+        out_shape=jax.ShapeDtypeStruct((rows, out_width), bf),
+        in_specs=[any_spec, vmem_spec, vmem_spec, any_spec, any_spec, any_spec, vmem_spec],
+        out_specs=vmem_spec,
+        scratch_shapes=[
+            pltpu.VMEM((3, rows, width), bf),
+            pltpu.VMEM((2, held, width), f32),
+            pltpu.VMEM(out_weight.shape, bf),
+            pltpu.VMEM((parts, 2 * rows, 2 * rows), bf),
+            pltpu.VMEM((3, 16, width), bf),
+            pltpu.VMEM((rows, width), f32),
+            pltpu.VMEM((rows, width), f32),
+            pltpu.VMEM((rows, width), bf),
+            pltpu.VMEM((parts, rows, LANES), bf),
+            pltpu.VMEM((2, held, width), bf),
+            pltpu.VMEM((groups, 2, held, LANES), bf),
+            pltpu.VMEM((parts, 2 * rows, LANES), bf),
+            pltpu.VMEM((parts, 2 * rows, LANES), f32),
+            pltpu.VMEM((parts, 2 * rows, LANES), f32),
+            pltpu.VMEM((parts, rows, LANES), bf),
+            pltpu.VMEM((parts, rows, LANES), bf),
+            pltpu.VMEM((rows, width), bf),
+            exchange, exchange, exchange, exchange, exchange, exchange,
+            dma((5,)), dma((2,)),
+            dma((parts,)), dma((parts,)),
+            dma((2, groups)), dma((2, groups)),
+            dma((parts,)), dma((parts,)),
+            dma((pieces,)), dma((pieces,)),
+            dma((pieces,)), dma((pieces,)),
+            dma((pieces,)), dma((pieces,)),
+        ],
+        compiler_params=pltpu.CompilerParams(
+            collective_id=0, has_side_effects=True, vmem_limit_bytes=56 * 1024 * 1024
+        ),
+    )(
+        projected,
+        short_taps.reshape(9, width),
+        skip_gain.reshape(1, width),
+        filter_response,
+        out_weight,
+        jnp.asarray(dft_tables(rows, parts)),
+        jnp.asarray(regroup_matrix(held, 2 * parts)),
+    )
 
 
 def shifted(value, axis, steps):
@@ -16,7 +381,7 @@
     return jnp.einsum(form, left, right, precision=lax.Precision.HIGHEST)
 
 
-def per_device(projected, short_taps, skip_gain, filter_response, out_weight):
+def per_device_collectives(projected, short_taps, skip_gain, filter_response, out_weight):
     seq_rows = projected.shape[1]
     seq_parts = lax.axis_size("seq")
     coarse_len = 2 * seq_parts
@@ -104,6 +469,21 @@
     )
 
 
+def per_device(projected, short_taps, skip_gain, filter_response, out_weight):
+    parts = lax.axis_size("seq")
+    rows, width = projected.shape[1:]
+    fits = (
+        parts == 8
+        and lax.axis_size("chan") == 4
+        and width == parts // 2 * LANES
+        and rows % 32 == 0
+        and filter_response.shape[1] == 2 * rows
+        and out_weight.shape[1] % (16 * LANES) == 0
+    )
+    form = per_device_kernel if fits else per_device_collectives
+    return form(projected, short_taps, skip_gain, filter_response, out_weight)
+
+
 def solution(mesh):
     placed = (
         P(None, "seq", "chan"),

time: 163 us -> 73.5 us (0.45)
  Pallas kernels: 0 us -> 68.7 us
  waiting for transfers between devices: 64.1 us -> 0 us
  matrix products: 28.6 us -> 0 us
  local copies, waits for them, and re-layouts: 22.3 us -> 3.67 us
  starting transfers between devices: 15.4 us -> 0 us
  between operations: 13.6 us -> 0.01 us
  blocking collectives: 12.3 us -> 0 us
  other arithmetic: 6.52 us -> 0 us
    pallas_call x0 -> x1, Pallas kernels: none -> 68.7 us  [per_device_kernel(): pl.pallas_call(functools.partial(layer_kernel, parts, pieces), out_shape=...]
    reduce_scatter x1 -> x0, waiting for transfers between devices: 43.7 us -> none  [per_device(): lax.psum_scatter(partial_terms.astype(jnp.bfloat16), 'chan', scatter_dime...]
    dot_general x9 -> x0, matrix products: 16.6 us -> none  [the longest x8 12.2 us: product_einsum(): return jnp.einsum(form, left, right, precision=lax.Precision.HIGHEST)]
    all_to_all x2 -> x0, waiting for transfers between devices: 14.3 us -> none  [the longest x1 10.1 us: per_device(): lax.all_to_all(filter_response.astype(jnp.bfloat16), 'seq', split_axis=2,...]
    all_to_all x1 -> x0, blocking collectives: 12.3 us -> none  [per_device(): lax.all_to_all(inverse_part.reshape(seq_parts * seq_rows, narrow_width).a...]
    unnamed x4 -> x0, matrix products: 11.9 us -> none
    all_to_all x2 -> x0, starting transfers between devices: 10.4 us -> none  [the longest x1 6.8 us: per_device(): lax.all_to_all(signal.astype(jnp.bfloat16), 'seq', split_axis=1, concat_a...]
    slice x6 -> x0, local copies, waits for them, and re-layouts: 8.19 us -> none  [the longest x3 6.31 us: per_device(): kept_real = spec_real * resp_grid[0] - spec_imag * resp_grid[1]]
  transfers between devices with their start and end apart: 4 -> 0, of which waited for: 4 -> 0; matrix products, arithmetic and copies ran while one was open for 13% -> 0% of each run, Pallas kernels for 0% -> 0%
where the time goes in v1:
time: 73.5 us; the launch traced here: 72.4 us
  Pallas kernels  68.7 us (93%)
  local copies, waits for them, and re-layouts  3.67 us (5%)
    pallas_call x1, Pallas kernels, per_device_kernel(): pl.pallas_call(functools.partial(layer_kernel, parts, pieces), out_shape=...  68.7 us
    unnamed x1, local copies, waits for them, and re-layouts  2.3 us

profile of v1, /device:TPU:0, one launch (start us, length us, event | category | flops | bytes accessed | tf_op | source)
XLA Modules:
  0.0 72.4 jit_solution(11705275047459006395)
XLA Ops:
  0.0 1.4 %reshape.6.taps_ref = f32[9,512]{1,0:T(8,128)} reshape(f32[3,3,512]{2,1,0:T(4,128)} %param.8) | data formatting | bytes 36864 | tf_op jit(solution)/shard_map/reshape | solution.py:365
  1.4 68.7 %shard_map.73 = bf16[256,2048]{1,0:T(8,128)(2,1)} custom-call(bf16[3,256,512]{2,1,0:T(8,128)(2,1)} %proj_hbm.1, f32[9,512]{1,0:T(8,128)} %reshape.6.taps_ref, f32[1,512]{1,0:T(1,128)} %bitcast.1, f32[2,512,512]{2,1,0:T(8,128)} %filt_hbm.1, bf16[512,8192]{1,0:T(8,128)(2,1)} %weight_hbm.1, bf16[8,512,512]{2,1,0:T(8,128)(2,1)} %constant.4.clone.tables_hbm, ...), custom_call_target="tpu_custom_call" | custom-call | tf_op jit(solution)/shard_map/pallas_call | solution.py:328
  70.0 2.3 %copy.9 = bf16[256,2048]{1,0:T(8,128)(2,1)} copy(bf16[256,2048]{1,0:T(8,128)(2,1)} %shard_map.73) | data formatting | bytes 2097152

commit v2 on v1

--- a/solution.py
+++ b/solution.py
@@ -63,15 +63,15 @@
 
 
 def layer_kernel(
-    parts, pieces,
-    proj_hbm, taps_ref, skip_ref, filt_hbm, weight_hbm, tables_hbm, regroup_ref,
+    parts, pieces, row_chunks,
+    proj_hbm, taps_ref, skip_ref, filt_hbm, weight_hbm, tables_hbm, regroup_hbm,
     out_ref,
-    proj, filt, weight, tables, rim,
+    proj, filt, weight, tables, regroup, rim,
     query, signal, signal_bf, heard, filt_bf, resp,
     coarse_in, spectrum, inverse, narrow_out, returned, gated,
-    side_out, side_in, far_out, far_in, side_own_out, side_own_in,
+    side_out, side_in, far_out, far_in, side_own_out, side_own_in, own_sum,
     load_sem, rim_sem, sig_send, sig_recv, filt_send, filt_recv,
-    back_send, back_recv, side_send, side_recv, far_send, far_recv, own_send, own_recv,
+    back_send, back_recv, side_sems, far_sems, own_sems,
 ):
     seq = lax.axis_index("seq")
     chan = lax.axis_index("chan")
@@ -88,25 +88,25 @@
     out_width = out_ref.shape[1]
     piece = out_width // pieces
 
+    barrier = pltpu.get_barrier_semaphore()
+    for o in range(1, parts):
+        pl.semaphore_signal(barrier, inc=1, device_id={"seq": (seq + o) % parts}, device_id_type=MESH)
+    for partner in (sibling, across):
+        pl.semaphore_signal(barrier, inc=1, device_id={"chan": partner}, device_id_type=MESH)
+
     load_proj = pltpu.make_async_copy(proj_hbm, proj, load_sem.at[0])
     load_proj.start()
+    load_regroup = pltpu.make_async_copy(regroup_hbm, regroup, load_sem.at[5])
+    load_regroup.start()
     load_filt = []
     for p in range(2):
         load_filt.append(pltpu.make_async_copy(filt_hbm.at[p], filt.at[p], load_sem.at[1 + p]))
         load_filt[-1].start()
     load_tables = pltpu.make_async_copy(tables_hbm, tables, load_sem.at[3])
-    load_tables.start()
     load_weight = pltpu.make_async_copy(weight_hbm, weight, load_sem.at[4])
-    load_weight.start()
-
-    barrier = pltpu.get_barrier_semaphore()
-    for o in range(1, parts):
-        pl.semaphore_signal(barrier, inc=1, device_id={"seq": (seq + o) % parts}, device_id_type=MESH)
-    for partner in (sibling, across):
-        pl.semaphore_signal(barrier, inc=1, device_id={"chan": partner}, device_id_type=MESH)
+
+    load_proj.wait()
     pl.semaphore_wait(barrier, parts + 1)
-
-    load_proj.wait()
     rim_copy = pltpu.make_async_remote_copy(
         src_ref=proj.at[:, pl.ds(rows - 16, 16), :],
         dst_ref=rim,
@@ -122,7 +122,7 @@
     def send_filter(p):
         load_filt[p].wait()
         filt_bf[p] = jnp.dot(
-            regroup_ref[...], filt[p].astype(jnp.bfloat16), preferred_element_type=jnp.float32
+            regroup[...], filt[p].astype(jnp.bfloat16), preferred_element_type=jnp.float32
         ).astype(jnp.bfloat16)
         for o in range(1, groups):
             target = (group + o) % groups
@@ -138,33 +138,43 @@
             copy.start()
             filt_copies.append(copy)
 
+    def shaped(i, columns, count, fixed):
+        now = proj[i, :count, columns].astype(jnp.float32)
+        one, two = pltpu.roll(now, 1, 0), pltpu.roll(now, 2, 0)
+        if fixed:
+            row_index = lax.broadcasted_iota(jnp.int32, now.shape, 0)
+            edge = rim[i, :, columns].astype(jnp.float32)
+            edge = jnp.where(seq == 0, jnp.zeros_like(edge), edge)
+            last, before = edge[15:16], edge[14:15]
+            one = jnp.where(row_index == 0, last, one)
+            two = jnp.where(row_index == 0, before, jnp.where(row_index == 1, last, two))
+        return (
+            taps_ref[i, 0:1, columns] * now
+            + taps_ref[i, 1:2, columns] * one
+            + taps_ref[i, 2:3, columns] * two
+        )
+
+    def shape_signal(count, fixed):
+        for g in range(groups):
+            columns = slice(g * LANES, (g + 1) * LANES)
+            value = shaped(1, columns, count, fixed) * shaped(2, columns, count, fixed)
+            signal[:count, columns] = value
+            signal_bf[:count, columns] = value.astype(jnp.bfloat16)
+
+    def shape_query(count, fixed):
+        for g in range(groups):
+            columns = slice(g * LANES, (g + 1) * LANES)
+            query[:count, columns] = shaped(0, columns, count, fixed)
+
+    shape_signal(rows, False)
+    load_regroup.wait()
     send_filter(0)
     rim_copy.wait()
-
-    row_index = lax.broadcasted_iota(jnp.int32, (rows, LANES), 0)
-
-    def shaped(i, columns):
-        now = proj[i, :, columns].astype(jnp.float32)
-        edge = rim[i, :, columns].astype(jnp.float32)
-        edge = jnp.where(seq == 0, jnp.zeros_like(edge), edge)
-        last, before = edge[15:16], edge[14:15]
-        one = jnp.where(row_index == 0, last, pltpu.roll(now, 1, 0))
-        two = jnp.where(row_index == 0, before, jnp.where(row_index == 1, last, pltpu.roll(now, 2, 0)))
-        return (
-            taps_ref[3 * i : 3 * i + 1, columns] * now
-            + taps_ref[3 * i + 1 : 3 * i + 2, columns] * one
-            + taps_ref[3 * i + 2 : 3 * i + 3, columns] * two
-        )
-
-    for g in range(groups):
-        columns = slice(g * LANES, (g + 1) * LANES)
-        product = shaped(1, columns) * shaped(2, columns)
-        signal[:, columns] = product
-        signal_bf[:, columns] = product.astype(jnp.bfloat16)
+    shape_signal(16, True)
 
     own_columns = pl.ds(pl.multiple_of(group * LANES, LANES), LANES)
     sig_copies = []
-    for o in range(1, parts):
+    for o in sorted(range(1, parts), key=lambda o: abs(o - groups)):
         target = (seq + o) % parts
         columns = pl.ds(pl.multiple_of((target % groups) * LANES, LANES), LANES)
         copy = pltpu.make_async_remote_copy(
@@ -179,11 +189,12 @@
         sig_copies.append(copy)
     heard[seq] = signal_bf[:, own_columns]
     send_filter(1)
+    load_tables.start()
+    load_weight.start()
     for p in range(2):
         resp[group, p] = filt_bf[p, :, own_columns]
-    for g in range(groups):
-        columns = slice(g * LANES, (g + 1) * LANES)
-        query[:, columns] = shaped(0, columns)
+    shape_query(rows, False)
+    shape_query(16, True)
 
     for copy in sig_copies:
         copy.wait_recv()
@@ -246,68 +257,78 @@
             narrow_out[n, pl.ds(start, chunk), :] = (weighted(terms) * sign).astype(jnp.bfloat16)
         return carry
 
-    lax.fori_loop(0, rows // chunk, backward, 0)
     back_copies = []
-    for o in range(1, parts):
-        target = (seq + o) % parts
-        copy = pltpu.make_async_remote_copy(
-            src_ref=narrow_out.at[target],
-            dst_ref=returned.at[seq],
-            send_sem=back_send.at[o],
-            recv_sem=back_recv.at[o],
-            device_id={"seq": target},
-            device_id_type=MESH,
-        )
-        copy.start()
-        back_copies.append(copy)
+    for t, (first, count) in enumerate(row_chunks):
+        lax.fori_loop(first // chunk, (first + count) // chunk, backward, 0)
+        here = pl.ds(first, count)
+        back_copies.append([])
+        for o in sorted(range(1, parts), key=lambda o: abs(o - groups)):
+            target = (seq + o) % parts
+            copy = pltpu.make_async_remote_copy(
+                src_ref=narrow_out.at[target, here],
+                dst_ref=returned.at[seq, here],
+                send_sem=back_send.at[t, o],
+                recv_sem=back_recv.at[t, o],
+                device_id={"seq": target},
+                device_id_type=MESH,
+            )
+            copy.start()
+            back_copies[t].append(copy)
     returned[seq] = narrow_out[seq]
     load_weight.wait()
-    for copy in back_copies:
-        copy.wait_recv()
-
-    for g in range(groups):
-        columns = slice(g * LANES, (g + 1) * LANES)
-        filtered = returned[g].astype(jnp.float32) + returned[groups + g].astype(jnp.float32)
-        gated[:, columns] = (
-            query[:, columns] * (filtered + skip_ref[:, columns] * signal[:, columns])
-        ).astype(jnp.bfloat16)
-
-    def product(block, c):
-        columns = pl.ds(pl.multiple_of(block * out_width + c * piece, piece), piece)
-        return jnp.dot(gated[...], weight[:, columns], preferred_element_type=jnp.float32)
-
-    def send(source, target_ref, send_sem, recv_sem, c, partner):
+
+    def send(source, target_ref, sems, at, part, partner):
+        rows_at, columns = part
         copy = pltpu.make_async_remote_copy(
-            src_ref=source.at[c],
-            dst_ref=target_ref.at[c],
-            send_sem=send_sem.at[c],
-            recv_sem=recv_sem.at[c],
+            src_ref=source.at[rows_at, columns],
+            dst_ref=target_ref.at[rows_at, columns],
+            send_sem=sems.at[0, at],
+            recv_sem=sems.at[1, at],
             device_id={"chan": partner},
             device_id_type=MESH,
         )
         copy.start()
         return copy
 
-    side_copies, far_copies, own_copies = [], [], []
-    for c in range(pieces):
-        side_out[c] = product(diagonal, c).astype(jnp.bfloat16)
-        side_copies.append(send(side_out, side_in, side_send, side_recv, c, sibling))
-    for c in range(pieces):
-        mine = product(across, c)
-        side_copies[c].wait_recv()
-        far_out[c] = (mine + side_in[c].astype(jnp.float32)).astype(jnp.bfloat16)
-        far_copies.append(send(far_out, far_in, far_send, far_recv, c, across))
-    for c in range(pieces):
-        side_own_out[c] = product(sibling, c).astype(jnp.bfloat16)
-        own_copies.append(send(side_own_out, side_own_in, own_send, own_recv, c, sibling))
-    for c in range(pieces):
-        mine = product(chan, c)
-        own_copies[c].wait_recv()
-        far_copies[c].wait_recv()
-        out_ref[:, c * piece : (c + 1) * piece] = (
-            mine + side_own_in[c].astype(jnp.float32) + far_in[c].astype(jnp.float32)
+    side_copies, far_copies, own_copies, all_parts = [], [], [], []
+    for t, (first, count) in enumerate(row_chunks):
+        for copy in back_copies[t]:
+            copy.wait_recv()
+        here = slice(first, first + count)
+        for g in range(groups):
+            columns = slice(g * LANES, (g + 1) * LANES)
+            filtered = returned[g, here].astype(jnp.float32) + returned[groups + g, here].astype(jnp.float32)
+            gated[here, columns] = (
+                query[here, columns] * (filtered + skip_ref[:, columns] * signal[here, columns])
+            ).astype(jnp.bfloat16)
+
+        def product(block, c):
+            columns = pl.ds(pl.multiple_of(block * out_width + c * piece, piece), piece)
+            return jnp.dot(gated[here], weight[:, columns], preferred_element_type=jnp.float32)
+
+        base = len(all_parts)
+        parts_here = [(pl.ds(first, count), pl.ds(c * piece, piece)) for c in range(pieces)]
+        all_parts += parts_here
+        for c, part in enumerate(parts_here):
+            side_out[part] = product(diagonal, c).astype(jnp.bfloat16)
+            side_copies.append(send(side_out, side_in, side_sems, base + c, part, sibling))
+        for c, part in enumerate(parts_here):
+            mine = product(across, c)
+            side_copies[base + c].wait_recv()
+            far_out[part] = (mine + side_in[part].astype(jnp.float32)).astype(jnp.bfloat16)
+            far_copies.append(send(far_out, far_in, far_sems, base + c, part, across))
+        for c, part in enumerate(parts_here):
+            side_own_out[part] = product(sibling, c).astype(jnp.bfloat16)
+            own_copies.append(send(side_own_out, side_own_in, own_sems, base + c, part, sibling))
+        for c, part in enumerate(parts_here):
+            own_sum[part] = product(chan, c)
+    for at, part in enumerate(all_parts):
+        own_copies[at].wait_recv()
+        far_copies[at].wait_recv()
+        out_ref[part] = (
+            own_sum[part] + side_own_in[part].astype(jnp.float32) + far_in[part].astype(jnp.float32)
         ).astype(jnp.bfloat16)
-    for copy in filt_copies + sig_copies + back_copies + side_copies + far_copies + own_copies:
+    for copy in filt_copies + sig_copies + sum(back_copies, []) + side_copies + far_copies + own_copies:
         copy.wait_send()
 
 
@@ -318,23 +339,26 @@
     held = filter_response.shape[1]
     out_width = out_weight.shape[1] // chans
     groups = parts // 2
-    pieces = 4
-    piece = out_width // pieces
+    pieces = 2
+    quarter = rows // 4
+    row_chunks = ((0, quarter), (quarter, quarter), (2 * quarter, 2 * quarter))
+    count = pieces * len(row_chunks)
     bf, f32 = jnp.bfloat16, jnp.float32
     any_spec = pl.BlockSpec(memory_space=pl.ANY)
     vmem_spec = pl.BlockSpec(memory_space=pltpu.VMEM)
     dma = pltpu.SemaphoreType.DMA
-    exchange = pltpu.VMEM((pieces, rows, piece), bf)
+    exchange = pltpu.VMEM((rows, out_width), bf)
     return pl.pallas_call(
-        functools.partial(layer_kernel, parts, pieces),
+        functools.partial(layer_kernel, parts, pieces, row_chunks),
         out_shape=jax.ShapeDtypeStruct((rows, out_width), bf),
-        in_specs=[any_spec, vmem_spec, vmem_spec, any_spec, any_spec, any_spec, vmem_spec],
+        in_specs=[any_spec, vmem_spec, vmem_spec, any_spec, any_spec, any_spec, any_spec],
         out_specs=vmem_spec,
         scratch_shapes=[
             pltpu.VMEM((3, rows, width), bf),
             pltpu.VMEM((2, held, width), f32),
             pltpu.VMEM(out_weight.shape, bf),
             pltpu.VMEM((parts, 2 * rows, 2 * rows), bf),
+            pltpu.VMEM((held, held), bf),
             pltpu.VMEM((3, 16, width), bf),
             pltpu.VMEM((rows, width), f32),
             pltpu.VMEM((rows, width), f32),
@@ -349,20 +373,19 @@
             pltpu.VMEM((parts, rows, LANES), bf),
             pltpu.VMEM((rows, width), bf),
             exchange, exchange, exchange, exchange, exchange, exchange,
-            dma((5,)), dma((2,)),
+            pltpu.VMEM((rows, out_width), f32),
+            dma((6,)), dma((2,)),
             dma((parts,)), dma((parts,)),
             dma((2, groups)), dma((2, groups)),
-            dma((parts,)), dma((parts,)),
-            dma((pieces,)), dma((pieces,)),
-            dma((pieces,)), dma((pieces,)),
-            dma((pieces,)), dma((pieces,)),
+            dma((len(row_chunks), parts)), dma((len(row_chunks), parts)),
+            dma((2, count)), dma((2, count)), dma((2, count)),
         ],
         compiler_params=pltpu.CompilerParams(
             collective_id=0, has_side_effects=True, vmem_limit_bytes=56 * 1024 * 1024
         ),
     )(
         projected,
-        short_taps.reshape(9, width),
+        short_taps,
         skip_gain.reshape(1, width),
         filter_response,
         out_weight,
@@ -476,7 +499,7 @@
         parts == 8
         and lax.axis_size("chan") == 4
         and width == parts // 2 * LANES
-        and rows % 32 == 0
+        and rows % 128 == 0
         and filter_response.shape[1] == 2 * rows
         and out_weight.shape[1] % (16 * LANES) == 0
     )

time: 73.5 us -> 67.2 us (0.914)
  Pallas kernels: 68.7 us -> 64.4 us
  local copies, waits for them, and re-layouts: 3.67 us -> 2.3 us
    pallas_call x1, Pallas kernels: 68.7 us -> 64.4 us  [per_device_kernel(): pl.pallas_call(functools.partial(layer_kernel, parts, pieces, row_chunks)...]
    reshape x1 -> x0, local copies, waits for them, and re-layouts: 1.36 us -> none  [per_device_kernel(): short_taps.reshape(9, width)]
where the time goes in v2:
time: 67.2 us; the launch traced here: 66.7 us
  Pallas kernels  64.4 us (96%)
  local copies, waits for them, and re-layouts  2.3 us (3%)
    pallas_call x1, Pallas kernels, per_device_kernel(): pl.pallas_call(functools.partial(layer_kernel, parts, pieces, row_chunks)...  64.4 us
    unnamed x1, local copies, waits for them, and re-layouts  2.3 us

profile of v2, /device:TPU:0, one launch (start us, length us, event | category | flops | bytes accessed | tf_op | source)
XLA Modules:
  0.0 66.7 jit_solution(6421886808013783096)
XLA Ops:
  0.0 64.4 %shard_map.73 = bf16[256,2048]{1,0:T(8,128)(2,1)} custom-call(bf16[3,256,512]{2,1,0:T(8,128)(2,1)} %proj_hbm.1, f32[3,3,512]{2,1,0:T(4,128)} %taps_ref.1, f32[1,512]{1,0:T(1,128)} %bitcast.1, f32[2,512,512]{2,1,0:T(8,128)} %filt_hbm.1, bf16[512,8192]{1,0:T(8,128)(2,1)} %weight_hbm.1, bf16[8,512,512]{2,1,0:T(8,128)(2,1)} %constant.4.clone.tables_hbm, ...), custom_call_target="tpu_custom_call" | custom-call | tf_op jit(solution)/shard_map/pallas_call | solution.py:351
  64.4 2.3 %copy.9 = bf16[256,2048]{1,0:T(8,128)(2,1)} copy(bf16[256,2048]{1,0:T(8,128)(2,1)} %shard_map.73) | data formatting | bytes 2097152

commit v3 on v2

--- a/solution.py
+++ b/solution.py
@@ -65,13 +65,13 @@
 def layer_kernel(
     parts, pieces, row_chunks,
     proj_hbm, taps_ref, skip_ref, filt_hbm, weight_hbm, tables_hbm, regroup_hbm,
-    out_ref,
+    out_hbm,
     proj, filt, weight, tables, regroup, rim,
     query, signal, signal_bf, heard, filt_bf, resp,
     coarse_in, spectrum, inverse, narrow_out, returned, gated,
-    side_out, side_in, far_out, far_in, side_own_out, side_own_in, own_sum,
+    side_out, side_in, far_out, far_in, side_own_out, side_own_in, own_sum, mixed,
     load_sem, rim_sem, sig_send, sig_recv, filt_send, filt_recv,
-    back_send, back_recv, side_sems, far_sems, own_sems,
+    back_send, back_recv, side_sems, far_sems, own_sems, store_sems,
 ):
     seq = lax.axis_index("seq")
     chan = lax.axis_index("chan")
@@ -85,7 +85,7 @@
     coarse = 2 * parts
     half_rows = rows // 2
     fine_held = filt.shape[1] // coarse
-    out_width = out_ref.shape[1]
+    out_width = mixed.shape[1]
     piece = out_width // pieces
 
     barrier = pltpu.get_barrier_semaphore()
@@ -258,8 +258,9 @@
         return carry
 
     back_copies = []
-    for t, (first, count) in enumerate(row_chunks):
-        lax.fori_loop(first // chunk, (first + count) // chunk, backward, 0)
+
+    def start_back(t):
+        first, count = row_chunks[t]
         here = pl.ds(first, count)
         back_copies.append([])
         for o in sorted(range(1, parts), key=lambda o: abs(o - groups)):
@@ -274,6 +275,18 @@
             )
             copy.start()
             back_copies[t].append(copy)
+
+    def next_back():
+        t = len(back_copies)
+        if t < len(row_chunks):
+            for copy in back_copies[t - 1]:
+                copy.wait_send()
+            start_back(t)
+
+    lax.fori_loop(0, row_chunks[0][1] // chunk, backward, 0)
+    start_back(0)
+    lax.fori_loop(row_chunks[0][1] // chunk, rows // chunk, backward, 0)
+    next_back()
     returned[seq] = narrow_out[seq]
     load_weight.wait()
 
@@ -317,19 +330,45 @@
             side_copies[base + c].wait_recv()
             far_out[part] = (mine + side_in[part].astype(jnp.float32)).astype(jnp.bfloat16)
             far_copies.append(send(far_out, far_in, far_sems, base + c, part, across))
+        next_back()
         for c, part in enumerate(parts_here):
             side_own_out[part] = product(sibling, c).astype(jnp.bfloat16)
             own_copies.append(send(side_own_out, side_own_in, own_sems, base + c, part, sibling))
         for c, part in enumerate(parts_here):
             own_sum[part] = product(chan, c)
+    stores = []
     for at, part in enumerate(all_parts):
         own_copies[at].wait_recv()
         far_copies[at].wait_recv()
-        out_ref[part] = (
+        mixed[part] = (
             own_sum[part] + side_own_in[part].astype(jnp.float32) + far_in[part].astype(jnp.float32)
         ).astype(jnp.bfloat16)
-    for copy in filt_copies + sig_copies + sum(back_copies, []) + side_copies + far_copies + own_copies:
+        stores.append(pltpu.make_async_copy(mixed.at[part], out_hbm.at[part], store_sems.at[at]))
+        stores[-1].start()
+    for copy in filt_copies + sig_copies + back_copies[-1] + side_copies + far_copies + own_copies:
         copy.wait_send()
+    for copy in stores:
+        copy.wait()
+
+
+def place_kernel(source, target, held, loads, stores):
+    slabs = loads.shape[0]
+    rows = source.shape[0] // slabs
+    steps = []
+    for i in range(slabs):
+        here = pl.ds(i * rows, rows)
+        steps.append(
+            (
+                pltpu.make_async_copy(source.at[here], held.at[here], loads.at[i]),
+                pltpu.make_async_copy(held.at[here], target.at[here], stores.at[i]),
+            )
+        )
+        steps[-1][0].start()
+    for load, store in steps:
+        load.wait()
+        store.start()
+    for load, store in steps:
+        store.wait()
 
 
 def per_device_kernel(projected, short_taps, skip_gain, filter_response, out_weight):
@@ -348,11 +387,11 @@
     vmem_spec = pl.BlockSpec(memory_space=pltpu.VMEM)
     dma = pltpu.SemaphoreType.DMA
     exchange = pltpu.VMEM((rows, out_width), bf)
-    return pl.pallas_call(
+    mixed = pl.pallas_call(
         functools.partial(layer_kernel, parts, pieces, row_chunks),
         out_shape=jax.ShapeDtypeStruct((rows, out_width), bf),
         in_specs=[any_spec, vmem_spec, vmem_spec, any_spec, any_spec, any_spec, any_spec],
-        out_specs=vmem_spec,
+        out_specs=any_spec,
         scratch_shapes=[
             pltpu.VMEM((3, rows, width), bf),
             pltpu.VMEM((2, held, width), f32),
@@ -374,11 +413,12 @@
             pltpu.VMEM((rows, width), bf),
             exchange, exchange, exchange, exchange, exchange, exchange,
             pltpu.VMEM((rows, out_width), f32),
+            pltpu.VMEM((rows, out_width), bf),
             dma((6,)), dma((2,)),
             dma((parts,)), dma((parts,)),
             dma((2, groups)), dma((2, groups)),
             dma((len(row_chunks), parts)), dma((len(row_chunks), parts)),
-            dma((2, count)), dma((2, count)), dma((2, count)),
+            dma((2, count)), dma((2, count)), dma((2, count)), dma((count,)),
         ],
         compiler_params=pltpu.CompilerParams(
             collective_id=0, has_side_effects=True, vmem_limit_bytes=56 * 1024 * 1024
@@ -392,6 +432,13 @@
         jnp.asarray(dft_tables(rows, parts)),
         jnp.asarray(regroup_matrix(held, 2 * parts)),
     )
+    return pl.pallas_call(
+        place_kernel,
+        out_shape=jax.ShapeDtypeStruct(mixed.shape, mixed.dtype),
+        in_specs=[any_spec],
+        out_specs=any_spec,
+        scratch_shapes=[pltpu.VMEM(mixed.shape, mixed.dtype), dma((4,)), dma((4,))],
+    )(mixed)
 
 
 def shifted(value, axis, steps):

time: 67.2 us -> 66 us (0.982)
  local copies, waits for them, and re-layouts: 2.3 us -> 0 us
  Pallas kernels: 64.4 us -> 65.8 us
    unnamed x1 -> x0, local copies, waits for them, and re-layouts: 2.3 us -> none
    pallas_call x0 -> x1, Pallas kernels: none -> 1.98 us  [per_device_kernel(): pl.pallas_call(place_kernel, out_shape=jax.ShapeDtypeStruct(mixed.shape,...]
where the time goes in v3:
time: 66 us; the launch traced here: 65.8 us
  Pallas kernels  65.8 us (100%)
    pallas_call x1, Pallas kernels, per_device_kernel(): pl.pallas_call(functools.partial(layer_kernel, parts, pieces, row_chunks)...  63.8 us
    pallas_call x1, Pallas kernels, per_device_kernel(): pl.pallas_call(place_kernel, out_shape=jax.ShapeDtypeStruct(mixed.shape,...  1.98 us

profile of v3, /device:TPU:0, one launch (start us, length us, event | category | flops | bytes accessed | tf_op | source)
XLA Modules:
  0.0 65.8 jit_solution(7957878825105966628)
XLA Ops:
  0.0 63.8 %shard_map.73.source = bf16[256,2048]{1,0:T(8,128)(2,1)} custom-call(bf16[3,256,512]{2,1,0:T(8,128)(2,1)} %proj_hbm.1, f32[3,3,512]{2,1,0:T(4,128)} %taps_ref.1, f32[1,512]{1,0:T(1,128)} %bitcast.1, f32[2,512,512]{2,1,0:T(8,128)} %filt_hbm.1, bf16[512,8192]{1,0:T(8,128)(2,1)} %weight_hbm.1, bf16[8,512,512]{2,1,0:T(8,128)(2,1)} %constant.4.clone.tables_hbm, ...), custom_call_target="tpu_custom_call" | custom-call | tf_op jit(solution)/shard_map/pallas_call | solution.py:390
  63.8 2.0 %shard_map.74 = bf16[256,2048]{1,0:T(8,128)(2,1)} custom-call(bf16[256,2048]{1,0:T(8,128)(2,1)} %shard_map.73.source), custom_call_target="tpu_custom_call" | custom-call | tf_op jit(solution)/shard_map/pallas_call | solution.py:435

commit v4 on v3

--- a/solution.py
+++ b/solution.py
@@ -64,9 +64,9 @@
 
 def layer_kernel(
     parts, pieces, row_chunks,
-    proj_hbm, taps_ref, skip_ref, filt_hbm, weight_hbm, tables_hbm, regroup_hbm,
+    proj_hbm, taps_ref, skip_ref, filt_hbm, weight_hbm, tables_hbm, turned_hbm, regroup_hbm,
     out_hbm,
-    proj, filt, weight, tables, regroup, rim,
+    proj, filt, weight, tables, turned, regroup, rim,
     query, signal, signal_bf, heard, filt_bf, resp,
     coarse_in, spectrum, inverse, narrow_out, returned, gated,
     side_out, side_in, far_out, far_in, side_own_out, side_own_in, own_sum, mixed,
@@ -190,6 +190,8 @@
     heard[seq] = signal_bf[:, own_columns]
     send_filter(1)
     load_tables.start()
+    load_turned = pltpu.make_async_copy(turned_hbm, turned, load_sem.at[6])
+    load_turned.start()
     load_weight.start()
     for p in range(2):
         resp[group, p] = filt_bf[p, :, own_columns]
@@ -227,6 +229,7 @@
     for m in range(parts):
         spectrum[m] = jnp.dot(tables[m], coarse_in[m], preferred_element_type=jnp.float32)
 
+    load_turned.wait()
     for copy in filt_copies:
         copy.wait_recv()
 
@@ -240,9 +243,7 @@
             resp_imag = jnp.concatenate([resp[g, 1, held] for g in range(groups)], 0).astype(jnp.float32)
             kept.append((real * resp_real - imag * resp_imag).astype(jnp.bfloat16))
             kept.append((real * resp_imag + imag * resp_real).astype(jnp.bfloat16))
-        inverse[m] = lax.dot_general(
-            tables[m], jnp.concatenate(kept, 0), (((0,), (0,)), ((), ())), preferred_element_type=jnp.float32
-        )
+        inverse[m] = jnp.dot(turned[m], jnp.concatenate(kept, 0), preferred_element_type=jnp.float32)
 
     def backward(step, carry):
         start = pl.multiple_of(step * chunk, chunk)
@@ -379,6 +380,7 @@
     out_width = out_weight.shape[1] // chans
     groups = parts // 2
     pieces = 2
+    tables = dft_tables(rows, parts)
     quarter = rows // 4
     row_chunks = ((0, quarter), (quarter, quarter), (2 * quarter, 2 * quarter))
     count = pieces * len(row_chunks)
@@ -390,12 +392,13 @@
     mixed = pl.pallas_call(
         functools.partial(layer_kernel, parts, pieces, row_chunks),
         out_shape=jax.ShapeDtypeStruct((rows, out_width), bf),
-        in_specs=[any_spec, vmem_spec, vmem_spec, any_spec, any_spec, any_spec, any_spec],
+        in_specs=[any_spec, vmem_spec, vmem_spec, any_spec, any_spec, any_spec, any_spec, any_spec],
         out_specs=any_spec,
         scratch_shapes=[
             pltpu.VMEM((3, rows, width), bf),
             pltpu.VMEM((2, held, width), f32),
             pltpu.VMEM(out_weight.shape, bf),
+            pltpu.VMEM((parts, 2 * rows, 2 * rows), bf),
             pltpu.VMEM((parts, 2 * rows, 2 * rows), bf),
             pltpu.VMEM((held, held), bf),
             pltpu.VMEM((3, 16, width), bf),
@@ -414,7 +417,7 @@
             exchange, exchange, exchange, exchange, exchange, exchange,
             pltpu.VMEM((rows, out_width), f32),
             pltpu.VMEM((rows, out_width), bf),
-            dma((6,)), dma((2,)),
+            dma((7,)), dma((2,)),
             dma((parts,)), dma((parts,)),
             dma((2, groups)), dma((2, groups)),
             dma((len(row_chunks), parts)), dma((len(row_chunks), parts)),
@@ -429,7 +432,8 @@
         skip_gain.reshape(1, width),
         filter_response,
         out_weight,
-        jnp.asarray(dft_tables(rows, parts)),
+        jnp.asarray(tables),
+        jnp.asarray(np.ascontiguousarray(tables.transpose(0, 2, 1))),
         jnp.asarray(regroup_matrix(held, 2 * parts)),
     )
     return pl.pallas_call(

time: 66 us -> 66 us (level)
  no operation moved by 1% of the time
where the time goes in v4:
time: 66 us; the launch traced here: 65.8 us
  Pallas kernels  65.8 us (100%)
    pallas_call x1, Pallas kernels, per_device_kernel(): pl.pallas_call(functools.partial(layer_kernel, parts, pieces, row_chunks)...  63.8 us
    pallas_call x1, Pallas kernels, per_device_kernel(): pl.pallas_call(place_kernel, out_shape=jax.ShapeDtypeStruct(mixed.shape,...  1.98 us

profile of v4, /device:TPU:0, one launch (start us, length us, event | category | flops | bytes accessed | tf_op | source)
XLA Modules:
  0.0 65.8 jit_solution(11509957590851760424)
XLA Ops:
  0.0 63.8 %shard_map.82.source = bf16[256,2048]{1,0:T(8,128)(2,1)} custom-call(bf16[3,256,512]{2,1,0:T(8,128)(2,1)} %proj_hbm.1, f32[3,3,512]{2,1,0:T(4,128)} %taps_ref.1, f32[1,512]{1,0:T(1,128)} %bitcast.1, f32[2,512,512]{2,1,0:T(8,128)} %filt_hbm.1, bf16[512,8192]{1,0:T(8,128)(2,1)} %weight_hbm.1, bf16[8,512,512]{2,1,0:T(8,128)(2,1)} %constant.6.clone.tables_hbm, ...), custom_call_target="tpu_custom_call" | custom-call | tf_op jit(solution)/shard_map/pallas_call | solution.py:392
  63.8 2.0 %shard_map.83 = bf16[256,2048]{1,0:T(8,128)(2,1)} custom-call(bf16[256,2048]{1,0:T(8,128)(2,1)} %shard_map.82.source), custom_call_target="tpu_custom_call" | custom-call | tf_op jit(solution)/shard_map/pallas_call | solution.py:439
